TPU v7x, 256 devices: a whole 4x4x8 slice. The times are simulated.
256 devices in a mesh: ctx: 32 (over z, x), dp: 8 (over y, core).
Axes of the slice: x: 4, y: 4, z: 8, core: 2. Of those that a mesh axis runs over, the one named last changes fastest.
Arguments:
- queries: bfloat16 [8, 8192, 1024], P('dp', 'ctx'), may hold values from -8 to 8
- keys: bfloat16 [8, 8192, 1024], P('dp', 'ctx'), may hold values from -8 to 8
- values: bfloat16 [8, 8192, 1024], P('dp', 'ctx'), may hold values from -6 to 6
- cotangent: bfloat16 [8, 8192, 2048], P('dp', 'ctx'), may hold values from -6 to 6
- proj_weight: bfloat16 [1024, 2048], P('dp'), may hold values from -0.1875 to 0.1875
- pattern: int32 [8, 8, 64, 2], P('dp'), may hold values 0 or 1
Outputs:
- projected: bfloat16 [8, 8192, 2048], P('dp', 'ctx')
- grad_query: bfloat16 [8, 8192, 1024], P('dp', 'ctx')
- grad_key: bfloat16 [8, 8192, 1024], P('dp', 'ctx')
- grad_value: bfloat16 [8, 8192, 1024], P('dp', 'ctx')
- grad_proj: float32 [1024, 2048], P('dp', 'ctx')
Inputs may be any that keep to these rules, and one draw needn't show every extreme that they name: `pattern`: entries with o = 0 or with q - o < 1 are not read.
All inputs are finite; a program needn't handle non-finite values. No bound on the sum of `pattern` on one device may be relied on, other than what follows from the above.
Results may differ from a plain program's by a relative error of at most 0.0085.
The roundings to bfloat16 on the way count: a program that leaves them out, or rounds other values in their place, can miss the bound.
Values may be sent and summed in bfloat16 or wider, within the bound.
A program may use at most 128 MiB of HBM per device.

v0:
```python
import jax
import jax.numpy as jnp
from jax import lax
from jax.sharding import PartitionSpec as P

HEADS = 8
HDIM = 128
BLK = 128
BLK_DEV = 2
WIN = 2


masked_value = -1e30


def shifted(value, axis, steps):
    count = lax.axis_size(axis)
    leading, last = (max(0, -steps), min(count, count - steps))
    return lax.ppermute(value, axis, [(source, source + steps) for source in range(leading, last)])


def spread(block, axis, holder):
    block = jnp.where(lax.axis_index(axis) == holder, block, jnp.zeros_like(block))
    return lax.psum(block, axis)


def product(form, left, right):
    return jnp.einsum(form, left, right, preferred_element_type=jnp.float32)


def block_masks(pattern_rows, query_blocks):
    column = jnp.arange(WIN * BLK, dtype=jnp.int32)
    within = jnp.arange(BLK, dtype=jnp.int32)
    offsets = WIN - 1 - jnp.arange(WIN, dtype=jnp.int32)
    flipped = jnp.flip(pattern_rows, axis=2) == 1
    key_blocks = query_blocks[:, None] - offsets[None, :]
    permitted = (flipped | (offsets == 0)[None, None, :]) & (key_blocks >= 1)[:, None, :]
    expanded = jnp.repeat(permitted, BLK, axis=2)
    causal = (column[None, :] < (WIN - 1) * BLK) | (
        column[None, :] - (WIN - 1) * BLK <= within[:, None]
    )
    key_mask = expanded[:, :, None, :] & causal[None, None, :, :]
    sink_mask = (query_blocks[:, None, None] > 0) | (within[None, None, :] <= within[None, :, None])
    return (key_mask, sink_mask[:, None, :, :])


def attend_scores(queries_b, key_window, sink_keys, key_mask, sink_mask):
    inverse_root = HDIM ** (-0.5)
    scores = product("nqhd,nkhd->nhqk", queries_b, key_window) * inverse_root
    sink_scores = product("nqhd,khd->nhqk", queries_b, sink_keys) * inverse_root
    return (
        jnp.where(key_mask, scores, masked_value),
        jnp.where(sink_mask, sink_scores, masked_value),
    )


def forward_blocks(
    queries_b, key_window, value_window, sink_keys, sink_values, key_mask, sink_mask
):
    scores, sink_scores = attend_scores(queries_b, key_window, sink_keys, key_mask, sink_mask)
    row_max = jnp.maximum(jnp.max(scores, axis=-1), jnp.max(sink_scores, axis=-1))
    row_total = jnp.sum(jnp.exp(scores - row_max[..., None]), axis=-1) + jnp.sum(
        jnp.exp(sink_scores - row_max[..., None]), axis=-1
    )
    log_total = row_max + jnp.log(row_total)
    weights = jnp.exp(scores - log_total[..., None]).astype(jnp.bfloat16)
    sink_weights = jnp.exp(sink_scores - log_total[..., None]).astype(jnp.bfloat16)
    attended = product("nhqk,nkhd->nqhd", weights, value_window) + product(
        "nhqk,khd->nqhd", sink_weights, sink_values
    )
    return (attended.astype(jnp.bfloat16), log_total)


def backward_blocks(
    queries_b,
    key_window,
    value_window,
    sink_keys,
    sink_values,
    key_mask,
    sink_mask,
    log_total,
    out_grad,
    row_delta,
):
    inverse_root = HDIM ** (-0.5)
    scores, sink_scores = attend_scores(queries_b, key_window, sink_keys, key_mask, sink_mask)
    weights = jnp.exp(scores - log_total[..., None])
    sink_weights = jnp.exp(sink_scores - log_total[..., None])
    prob_grad = product("nqhd,nkhd->nhqk", out_grad, value_window)
    sink_prob_grad = product("nqhd,khd->nhqk", out_grad, sink_values)
    score_grad = (weights * (prob_grad - row_delta[..., None])).astype(jnp.bfloat16)
    sink_score_grad = (sink_weights * (sink_prob_grad - row_delta[..., None])).astype(jnp.bfloat16)
    query_grad = inverse_root * (
        product("nhqk,nkhd->nqhd", score_grad, key_window)
        + product("nhqk,khd->nqhd", sink_score_grad, sink_keys)
    )
    window_key_grad = inverse_root * product("nhqk,nqhd->nkhd", score_grad, queries_b)
    window_value_grad = product("nhqk,nqhd->nkhd", weights.astype(jnp.bfloat16), out_grad)
    sink_key_grad = inverse_root * product("nhqk,nqhd->khd", sink_score_grad, queries_b)
    sink_value_grad = product("nhqk,nqhd->khd", sink_weights.astype(jnp.bfloat16), out_grad)
    return (query_grad, window_key_grad, window_value_grad, sink_key_grad, sink_value_grad)


def make_windows(extended, first):
    pieces = [
        extended[(number + first) * BLK : (number + first + WIN) * BLK] for number in range(BLK_DEV)
    ]
    return jnp.stack(pieces).reshape(BLK_DEV, WIN * BLK, HEADS, HDIM)


def place_windows(window_grad):
    flat = window_grad.reshape(BLK_DEV, WIN * BLK, HEADS * HDIM)
    placed = jnp.zeros((2 * BLK_DEV * BLK, HEADS * HDIM), jnp.float32)
    for number in range(BLK_DEV):
        placed = placed + jnp.pad(
            flat[number], (((number + 1) * BLK, (2 * BLK_DEV - number - 1 - WIN) * BLK), (0, 0))
        )
    return placed


def body(queries, keys, values, cotangent, proj_weight, pattern):
    query_rows = queries[0]
    key_rows = keys[0]
    value_rows = values[0]
    grad_output = cotangent[0]
    pattern_doc = pattern[0]
    rows = query_rows.shape[0]
    width_heads = query_rows.shape[1]
    context_index = lax.axis_index("ctx")
    context_count = lax.axis_size("ctx")
    document_count = lax.axis_size("dp")
    prev_keys, prev_values = shifted((key_rows, value_rows), "ctx", 1)
    first_keys, first_values = (
        spread(key_rows[:BLK], "ctx", 0),
        spread(value_rows[:BLK], "ctx", 0),
    )
    full_weight = lax.all_gather(proj_weight, "dp", axis=0, tiled=True)
    query_blocks = context_index * BLK_DEV + jnp.arange(BLK_DEV, dtype=jnp.int32)
    pattern_rows = jnp.transpose(
        lax.dynamic_slice_in_dim(pattern_doc, context_index * BLK_DEV, BLK_DEV, 1), (1, 0, 2)
    )
    key_mask, sink_mask = block_masks(pattern_rows, query_blocks)
    key_window = make_windows(jnp.concatenate([prev_keys, key_rows], axis=0), 1)
    value_window = make_windows(jnp.concatenate([prev_values, value_rows], axis=0), 1)
    query_blocked = query_rows.reshape(BLK_DEV, BLK, HEADS, HDIM)
    sink_keys = first_keys.reshape(BLK, HEADS, HDIM)
    sink_values = first_values.reshape(BLK, HEADS, HDIM)
    attended, log_total = forward_blocks(
        query_blocked, key_window, value_window, sink_keys, sink_values, key_mask, sink_mask
    )
    attended_rows = attended.reshape(rows, width_heads)
    projected = jnp.dot(attended_rows, full_weight, preferred_element_type=jnp.float32).astype(
        jnp.bfloat16
    )
    grad_attended = lax.dot_general(
        grad_output, full_weight, (((1,), (1,)), ((), ())), preferred_element_type=jnp.float32
    ).astype(jnp.bfloat16)
    weight_scale = float(rows * context_count * document_count) ** (-0.5)
    weight_term = (
        lax.dot_general(
            attended_rows, grad_output, (((0,), (0,)), ((), ())), preferred_element_type=jnp.float32
        )
        * weight_scale
    )
    partial_sum = lax.psum_scatter(weight_term, "ctx", scatter_dimension=1, tiled=True)
    grad_proj = lax.psum_scatter(partial_sum, "dp", scatter_dimension=0, tiled=True)
    row_delta = jnp.sum(
        grad_attended.astype(jnp.float32).reshape(rows, HEADS, HDIM)
        * attended_rows.astype(jnp.float32).reshape(rows, HEADS, HDIM),
        axis=-1,
    )
    delta_blocked = jnp.transpose(row_delta.reshape(BLK_DEV, BLK, HEADS), (0, 2, 1))
    grad_blocked = grad_attended.reshape(BLK_DEV, BLK, HEADS, HDIM)
    query_grad, window_key, window_value, sink_key, sink_value = backward_blocks(
        query_blocked,
        key_window,
        value_window,
        sink_keys,
        sink_values,
        key_mask,
        sink_mask,
        log_total,
        grad_blocked,
        delta_blocked,
    )
    sink_key_sum, sink_value_sum = lax.psum((sink_key, sink_value), "ctx")
    placed_keys = place_windows(window_key)
    placed_values = place_windows(window_value)
    later_keys, later_values = shifted((placed_keys[:rows], placed_values[:rows]), "ctx", -1)
    own_key = placed_keys[rows:] + later_keys
    own_value = placed_values[rows:] + later_values
    leading = (context_index == 0).astype(jnp.float32)
    own_key = jnp.concatenate(
        [own_key[:BLK] + leading * sink_key_sum.reshape(BLK, width_heads), own_key[BLK:]], axis=0
    )
    own_value = jnp.concatenate(
        [own_value[:BLK] + leading * sink_value_sum.reshape(BLK, width_heads), own_value[BLK:]],
        axis=0,
    )
    return (
        projected[None],
        query_grad.reshape(rows, width_heads).astype(jnp.bfloat16)[None],
        own_key.astype(jnp.bfloat16)[None],
        own_value.astype(jnp.bfloat16)[None],
        grad_proj,
    )


def solution(mesh):
    return jax.shard_map(
        body,
        mesh=mesh,
        in_specs=(
            P("dp", "ctx", None),
            P("dp", "ctx", None),
            P("dp", "ctx", None),
            P("dp", "ctx", None),
            P("dp", None),
            P("dp", None, None, None),
        ),
        out_specs=(
            P("dp", "ctx", None),
            P("dp", "ctx", None),
            P("dp", "ctx", None),
            P("dp", "ctx", None),
            P("dp", "ctx"),
        ),
        check_vma=False,
    )
```

profile of v0, /device:TPU:14, one launch (start us, length us, event | category | flops | bytes accessed | tf_op | source)
XLA Modules:
  0.0 603.2 jit_solution(17470809247560676850)
XLA Ops:
  13.1 3.7 collective-permute-start
  16.8 3.4 collective-permute-start.1
  24.3 6.2 %collective-permute-done = bf16[256,1024]{0,1:T(8,128)(2,1)} collective-permute-done((bf16[256,1024]{0,1:T(8,128)(2,1)S(1)}, bf16[256,1024]{0,1:T(8,128)(2,1)}, u32[]{:S(2)}, u32[]{:S(2)}) %collective-permute-start) | collective-permute-done | bytes 524320 | tf_op jit(solution)/shard_map/ppermute | solution.py:19
  32.5 9.1 %collective-permute-done.1 = bf16[256,1024]{0,1:T(8,128)(2,1)} collective-permute-done((bf16[256,1024]{0,1:T(8,128)(2,1)S(1)}, bf16[256,1024]{0,1:T(8,128)(2,1)}, u32[]{:S(2)}, u32[]{:S(2)}) %collective-permute-start.1) | collective-permute-done | bytes 524320 | tf_op jit(solution)/shard_map/ppermute | solution.py:19
  43.6 118.1 %all-reduce.11.cloned.1.call-done = (bf16[128,8,128]{2,0,1:T(8,128)(2,1)}, bf16[128,8,128]{2,0,1:T(8,128)(2,1)}) async-done(((bf16[128,8,128]{2,0,1:T(8,128)(2,1)}, bf16[128,8,128]{2,0,1:T(8,128)(2,1)}), (bf16[128,8,128]{2,0,1:T(8,128)(2,1)}, bf16[128,8,128]{2,0,1:T(8,128)(2,1)})) %all-reduce.11.cloned.1.call-update) | async-done | bytes 524304 | tf_op jit(solution)/shard_map/psum | solution.py:24
  163.0 2.4 fusion.48
  170.0 3.5 convolution_convert_fusion.1
  175.9 2.1 copy.174
  178.8 2.6 convolution_bitcast_fusion.6
  185.9 4.6 convolution_multiply_fusion
  190.7 2.1 copy.172
  192.9 2.0 multiply_convert_fusion
  198.1 2.1 copy.164
  200.2 2.1 convert_element_type.79
  202.3 1.8 multiply_bitcast_fusion
  204.1 1.5 fusion.47
  205.6 2.6 copy.169
  208.2 2.5 copy.168
  210.7 2.1 pad_add_fusion.1
  212.8 2.8 collective-permute-start.2
  217.4 3.0 collective-permute-start.3
  220.5 2.2 fusion
  222.7 112.2 %all-reduce.9.cloned.1.call-done = (f32[128,8,128]{2,0,1:T(8,128)}, f32[128,8,128]{2,0,1:T(8,128)}) async-done(((f32[128,8,128]{2,0,1:T(8,128)}, f32[128,8,128]{2,0,1:T(8,128)}), (f32[128,8,128]{2,0,1:T(8,128)}, f32[128,8,128]{2,0,1:T(8,128)})) %all-reduce.9.cloned.1.call-update) | async-done | bytes 1048592 | tf_op jit(solution)/shard_map/psum | solution.py:187
  335.0 1.9 broadcast_multiply_fusion.1
  336.8 2.0 copy.171
  338.9 1.4 fusion.15
  341.3 2.0 copy.178
  343.3 1.9 broadcast_multiply_fusion
  345.2 2.0 copy.177
  347.3 2.4 fusion.17
  349.7 217.0 %reduce-scatter.3.cloned.1.call-done = f32[1024,64]{0,1:T(8,128)} async-done(((f32[1024,2048]{0,1:T(8,128)}), f32[1024,64]{0,1:T(8,128)}) %reduce-scatter.3.cloned.1.call-update) | async-done | bytes 262160 | tf_op jit(solution)/shard_map/reduce_scatter | solution.py:166
  570.1 25.9 %reduce-scatter.5.cloned.1.call-done = f32[128,64]{0,1:T(8,128)} async-done(((f32[1024,64]{0,1:T(8,128)}), f32[128,64]{0,1:T(8,128)}) %reduce-scatter.5.cloned.1.call-update) | async-done | bytes 32784 | tf_op jit(solution)/shard_map/reduce_scatter | solution.py:167
  (134 shorter events, 36.1 us)
Async XLA Ops:
  8.0 162.0 %copy-start = (bf16[1,256,2048]{2,1,0:T(8,128)(2,1)S(1)}, bf16[1,256,2048]{2,1,0:T(8,128)(2,1)}, u32[]{:S(2)}) copy-start(bf16[1,256,2048]{2,1,0:T(8,128)(2,1)} %param.9) | copy-start | bytes 3145732
  8.0 153.7 %all-reduce.11.cloned.1.call-start = ((), (), s32[]{:S(2)}) async-start(), calls=%async_computation.6 | async-start | bytes 1048576 | tf_op jit(solution)/shard_map/psum | solution.py:24
  10.6 10.6 %copy-start.27 = (bf16[1,256,1024]{2,1,0:T(8,128)(2,1)S(1)}, bf16[1,256,1024]{2,1,0:T(8,128)(2,1)}, u32[]{:S(2)}) copy-start(bf16[1,256,1024]{2,1,0:T(8,128)(2,1)} %param.6) | copy-start | bytes 1572868
  12.5 157.5 %all-gather.2.cloned.1.call-start = ((), (), s32[]{:S(2)}) async-start(), calls=%async_computation.2 | async-start | bytes 4718592 | tf_op jit(solution)/shard_map/all_gather | solution.py:138
  13.0 321.9 %all-reduce.9.cloned.1.call-start = ((), (), s32[]{:S(2)}) async-start(), calls=%async_computation.5 | async-start | bytes 2097152 | tf_op jit(solution)/shard_map/psum | solution.py:187
  13.1 17.4 %collective-permute-start = (bf16[256,1024]{0,1:T(8,128)(2,1)S(1)}, bf16[256,1024]{0,1:T(8,128)(2,1)}, u32[]{:S(2)}, u32[]{:S(2)}) collective-permute-start(bf16[256,1024]{0,1:T(8,128)(2,1)S(1)} %bitcast.149), channel_id=1, source_target_pairs={{0,8},{8,16},{16,24},{24,32},{32,40},{40,48},{48,56},{56,64},{64,7... | collective-permute-start | bytes 1572872 | tf_op jit(solution)/shard_map/ppermute | solution.py:19
  16.8 24.8 %collective-permute-start.1 = (bf16[256,1024]{0,1:T(8,128)(2,1)S(1)}, bf16[256,1024]{0,1:T(8,128)(2,1)}, u32[]{:S(2)}, u32[]{:S(2)}) collective-permute-start(bf16[256,1024]{0,1:T(8,128)(2,1)S(1)} %bitcast.146), channel_id=1, source_target_pairs={{0,8},{8,16},{16,24},{24,32},{32,40},{40,48},{48,56},{56,64},{64,7... | collective-permute-start | bytes 1572872 | tf_op jit(solution)/shard_map/ppermute | solution.py:19
  20.3 3.3 copy-start.29
  21.4 140.4 %copy-start.10 = (bf16[32,8,8,128]{3,2,1,0:T(8,128)(2,1)}, bf16[32,8,8,128]{3,2,1,0:T(8,128)(2,1)S(1)}, u32[]{:S(2)}) copy-start(bf16[32,8,8,128]{3,2,1,0:T(8,128)(2,1)S(1)} %copy.199) | copy-start | bytes 1572868
  163.0 4.2 copy-start.1
  165.4 1.2 copy-start.17
  173.5 1.4 copy-start.19
  178.0 3.4 copy-start.2
  178.0 3.4 copy-start.18
  178.8 3.7 copy-start.11
  183.6 383.0 %reduce-scatter.3.cloned.1.call-start = ((), (), s32[]{:S(2)}) async-start(), calls=%async_computation.3 | async-start | bytes 8650752 | tf_op jit(solution)/shard_map/reduce_scatter | solution.py:166
  190.5 2.4 copy-start.28
  190.5 405.6 %reduce-scatter.5.cloned.1.call-start = ((), (), s32[]{:S(2)}) async-start(), calls=%async_computation.4 | async-start | bytes 294912 | tf_op jit(solution)/shard_map/reduce_scatter | solution.py:167
  192.9 3.0 copy-start.23
  192.9 3.0 copy-start.24
  210.7 5.0 copy-start.12
  212.8 126.0 %collective-permute-start.2 = (f32[256,1024]{0,1:T(8,128)}, f32[256,1024]{0,1:T(8,128)}, u32[]{:S(2)}, u32[]{:S(2)}) collective-permute-start(f32[256,1024]{0,1:T(8,128)} %pad_add_fusion.1), channel_id=1, source_target_pairs={{8,0},{16,8},{24,16},{32,24},{40,32},{48,40},{56,48},{64,56},{72,6... | collective-permute-start | bytes 3145736 | tf_op jit(solution)/shard_map/ppermute | solution.py:19
  216.1 4.3 copy-start.30
  216.3 4.1 copy-start.6
  216.4 4.1 copy-start.8
  216.4 4.1 copy-start.21
  217.4 129.8 %collective-permute-start.3 = (f32[256,1024]{0,1:T(8,128)}, f32[256,1024]{0,1:T(8,128)}, u32[]{:S(2)}, u32[]{:S(2)}) collective-permute-start(f32[256,1024]{0,1:T(8,128)} %pad_add_fusion), channel_id=1, source_target_pairs={{8,0},{16,8},{24,16},{32,24},{40,32},{48,40},{56,48},{64,56},{72,6... | collective-permute-start | bytes 3145736 | tf_op jit(solution)/shard_map/ppermute | solution.py:19
  222.7 116.2 %copy-start.4 = (f32[1,256,8,128]{1,3,2,0:T(8,128)S(1)}, f32[1,256,8,128]{1,3,2,0:T(8,128)}, u32[]{:S(2)}) copy-start(f32[1,256,8,128]{1,3,2,0:T(8,128)} %copy.169) | copy-start | bytes 3145732
  222.7 116.2 %copy-start.5 = (f32[1,256,8,128]{1,3,2,0:T(8,128)S(1)}, f32[1,256,8,128]{1,3,2,0:T(8,128)}, u32[]{:S(2)}) copy-start(f32[1,256,8,128]{1,3,2,0:T(8,128)} %copy.168) | copy-start | bytes 3145732
  338.9 1.5 copy-start.22
  340.4 6.8 %copy-start.7 = (f32[1,256,8,128]{1,3,2,0:T(8,128)S(1)}, f32[1,256,8,128]{1,3,2,0:T(8,128)}, u32[]{:S(2)}) copy-start(f32[1,256,8,128]{1,3,2,0:T(8,128)} %copy-done.6) | copy-start | bytes 3145732
  340.4 6.8 %copy-start.9 = (f32[1,256,8,128]{1,3,2,0:T(8,128)S(1)}, f32[1,256,8,128]{1,3,2,0:T(8,128)}, u32[]{:S(2)}) copy-start(f32[1,256,8,128]{1,3,2,0:T(8,128)} %copy-done.8) | copy-start | bytes 3145732
  (8 other events, 7.5 us)
Sparse Core Ops, SparseCore 0:
  12.9 148.8 all-reduce.10
  183.8 151.1 all-reduce.8
  339.5 227.1 reduce-scatter.2
Sparse Core Ops, SparseCore 1:
  14.8 36.3 all-gather.1
  566.8 29.2 reduce-scatter.4
where the time goes:
time: 608 us; the launch traced here: 603 us
  waiting for transfers between devices  489 us (80%)
  local copies, waits for them, and re-layouts  43.7 us (7%)
  matrix products  24.8 us (4%)
  other arithmetic  16.5 us (3%)
  between operations  15.7 us (3%)
  starting transfers between devices  13.3 us (2%)
    reduce_scatter x1, waiting for transfers between devices, body(): lax.psum_scatter(weight_term, 'ctx', scatter_dimension=1, tiled=True)  217 us
    psum x1, waiting for transfers between devices, spread(): return lax.psum(block, axis)  118 us
    psum x1, waiting for transfers between devices, body(): sink_key_sum, sink_value_sum = lax.psum((sink_key, sink_value), 'ctx')  112 us
    reduce_scatter x1, waiting for transfers between devices, body(): lax.psum_scatter(partial_sum, 'dp', scatter_dimension=0, tiled=True)  25.9 us
    ppermute x4, waiting for transfers between devices, shifted(): lax.ppermute(value, axis, [(source, source + steps) for source in range(l...  15.3 us
    dot_general x12, matrix products, product(): return jnp.einsum(form, left, right, preferred_element_type=jnp.float32)  14.5 us
    ppermute x4, starting transfers between devices, shifted(): lax.ppermute(value, axis, [(source, source + steps) for source in range(l...  12.9 us
  transfers between devices with their start and end apart: 9, of which 6 were waited for; matrix products, arithmetic and copies ran while one was open for 10% of the time, Pallas kernels for 0%

commit v1 on v0

v1 whole, which is shorter than its diff:
```python
import jax
import jax.numpy as jnp
from jax import lax
from jax.experimental import pallas as pl
from jax.experimental.pallas import tpu as pltpu
from jax.sharding import PartitionSpec as P

MESH = pl.DeviceIdType.MESH
NX, NY, NZ = 4, 4, 8
HEADS, HDIM, BLK = 8, 128, 128
BF, F32 = jnp.bfloat16, jnp.float32
MASKED = -1.0e30
UNROLL = 4
SCALE = HDIM ** -0.5
SCALE2 = SCALE * 1.4426950408889634


def lanes(index, size=128):
    return pl.ds(pl.multiple_of(index * size, size), size)


def dot(a, b, da, db):
    return lax.dot_general(a, b, (((da,), (db,)), ((), ())), preferred_element_type=F32)


def kernel(pat_ref, q_ref, k_ref, v_ref, cot_ref, w_ref,
           proj_ref, dq_ref, dk_ref, dv_ref, gp_ref,
           pat, q, cot, wfull, kv, ct, cot_peer, a2, attn_send, attn_all, grad, gate, bias, probs,
           acc, pg, pg_recv, sgk, gk1, gk1s, gk2, gk2s, gk3, sgv, gv1, gv1s, gv2, gv2s, gv3,
           ptb, xfwd, xmrg, xin, yfwd, ymrg, yin, s2x, s2y, r2x, r2y, red, r3,
           local, prev_s, prev_r, w_s, w_r, core_s, core_r, sk_s, sk_r, kz_s, kz_r, kx_s, kx_r, vz_s, vz_r,
           pg_s, pg_r, gk1_s, gk1_r, gk2_s, gk2_r, gk3_s, gk3_r, gv1_s, gv1_r, gv2_s, gv2_r, gv3_s, gv3_r,
           px_s, px_r, py_s, py_r, p2_s, p2_r, p3_s, p3_r):
    c = lax.axis_index("ctx")
    d = lax.axis_index("dp")
    x, z = lax.rem(c, NX), lax.div(c, NX)
    y, core = lax.div(d, 2), lax.rem(d, 2)

    def xpeer(o):
        return lax.rem(x + o, NX)

    def ypeer(o):
        return lax.rem(y + o, NY)

    def zpeer(o):
        return lax.rem(z + o, NZ)

    def at_x(xx):
        return (z * NX + xx, d)

    def at_z(zz):
        return (zz * NX + x, d)

    def at_y(yy):
        return (c, yy * 2 + core)

    other = 1 - core
    at_core = (c, y * 2 + other)
    has_next, has_prev = c < NX * NZ - 1, c > 0
    root, row0, col0 = c == 0, z == 0, x == 0
    pending = []

    def remote(src, dst, send, recv, device):
        return pltpu.make_async_remote_copy(src_ref=src, dst_ref=dst, send_sem=send, recv_sem=recv,
                                            device_id=device, device_id_type=MESH)

    def send(src, dst, send_sem, recv_sem, device, cond=None):
        copy = remote(src, dst, send_sem, recv_sem, device)
        pending.append((cond, copy))
        if cond is None:
            copy.start()
        else:
            pl.when(cond)(lambda: copy.start())

    def arrive(dst, recv_sem, cond=None):
        copy = remote(dst, dst, recv_sem, recv_sem, at_core)
        if cond is None:
            copy.wait_recv()
        else:
            pl.when(cond)(lambda: copy.wait_recv())

    own = pl.ds(2 * BLK, 2 * BLK)
    loads = [
        pltpu.make_async_copy(k_ref, kv.at[0, own], local.at[0]),
        pltpu.make_async_copy(v_ref, kv.at[1, own], local.at[1]),
        pltpu.make_async_copy(w_ref, wfull.at[lanes(d)], local.at[2]),
        pltpu.make_async_copy(cot_ref, cot, local.at[3]),
        pltpu.make_async_copy(q_ref, q, local.at[4]),
        pltpu.make_async_copy(pat_ref, pat, local.at[5]),
    ]
    for load in loads:
        load.start()
    sink_loads = [
        pltpu.make_async_copy(k_ref.at[pl.ds(0, BLK)], kv.at[0, pl.ds(0, BLK)], local.at[6]),
        pltpu.make_async_copy(v_ref.at[pl.ds(0, BLK)], kv.at[1, pl.ds(0, BLK)], local.at[7]),
    ]
    for load in sink_loads:
        pl.when(root)(lambda load=load: load.start())

    barrier = pltpu.get_barrier_semaphore()

    def greet(device):
        pl.semaphore_signal(barrier, inc=1, device_id=device, device_id_type=MESH)

    for o in range(1, NZ):
        greet(at_z(zpeer(o)))
    for o in range(1, NX):
        greet(at_x(xpeer(o)))
    for o in range(1, NY):
        greet(at_y(ypeer(o)))
    greet(at_core)
    far_next = (x == NX - 1) & has_next
    far_prev = col0 & has_prev
    pl.when(far_next)(lambda: greet((c + 1, d)))
    pl.when(far_prev)(lambda: greet((c - 1, d)))
    pl.semaphore_wait(barrier, NX + NY + NZ - 2 + far_next.astype(jnp.int32) + far_prev.astype(jnp.int32))

    def krows(ref, xx):
        return ref.at[pl.ds(pl.multiple_of(xx * 32, 32), 32)]

    def vrows(ref, zz):
        return ref.at[pl.ds(pl.multiple_of(zz * 16, 16), 16)]

    skeys, svalues = kv.at[0], kv.at[1]

    def kchunk(xx, zz):
        return skeys.at[pl.ds(pl.multiple_of(xx * 32, 32), 32), lanes(zz)]

    for o in (2, 1, 3):
        send(k_ref.at[pl.ds(o * 32, 32)], skeys.at[pl.ds(o * 32, 32)], sk_s.at[o], sk_r.at[0], at_x(o), root)
    for o in (4, 5, 3, 6, 2, 7, 1):
        send(v_ref.at[pl.ds(o * 16, 16)], svalues.at[pl.ds(o * 16, 16)], sk_s.at[3 + o], sk_r.at[1], at_z(o), root)

    def wrows(dd, half):
        return wfull.at[pl.ds(pl.multiple_of(dd * 128 + half * 64, 64), 64)]

    up, down, opposite = ypeer(1), ypeer(3), ypeer(2)
    for way, half in ((0, 0), (1, 1), (0, 1), (1, 0)):
        send(w_ref.at[pl.ds(half * 64, 64)], wrows(d, half), w_s.at[way, half], w_r.at[way, half], at_y((up, down)[way]))
    send(k_ref.at[pl.ds(BLK, BLK)], kv.at[0, pl.ds(BLK, BLK)], prev_s.at[0], prev_r.at[0], (c + 1, d), has_next & (z > 0))
    send(cot_ref, cot_peer, core_s.at[1], core_r.at[1], at_core)
    send(w_ref, wfull.at[lanes(d)], core_s.at[0], core_r.at[0], at_core)

    arrive(krows(skeys, x), sk_r.at[0], row0 & has_prev)
    for oz in (4, 5, 3, 6, 2, 7, 1):
        send(skeys.at[pl.ds(pl.multiple_of(x * 32, 32), 32), pl.ds(oz * 128, 128)],
             kchunk(x, oz), kz_s.at[6 + oz], sk_r.at[2], at_z(oz), row0 & has_prev)
        send(k_ref.at[pl.ds(0, 32), pl.ds(oz * 128, 128)], kchunk(0, oz), kz_s.at[13 + oz], sk_r.at[2], at_z(oz), root)
    send(k_ref.at[pl.ds(BLK, BLK)], kv.at[0, pl.ds(BLK, BLK)], prev_s.at[2], prev_r.at[0], (c + 1, d), row0)
    arrive(vrows(svalues, z), sk_r.at[1], col0 & has_prev)
    for o in (2, 1, 3):
        send(vrows(svalues, z), vrows(svalues, z), vz_s.at[6 + o], sk_r.at[3], at_x(o), col0 & has_prev)
        send(v_ref.at[pl.ds(0, 16)], svalues.at[pl.ds(0, 16)], vz_s.at[9 + o], sk_r.at[3], at_x(o), root)

    arrive(vrows(svalues, z), sk_r.at[3], x > 0)
    send(v_ref.at[pl.ds(BLK, BLK)], kv.at[1, pl.ds(BLK, BLK)], prev_s.at[1], prev_r.at[1], (c + 1, d), has_next)

    for oz in (4, 5, 3, 6, 2, 7, 1):
        send(vrows(svalues, z), vrows(svalues, z), vz_s.at[oz - 1], vz_r.at[oz - 1], at_z(zpeer(oz)),
             has_prev & ((x > 0) | (zpeer(oz) > 0)))
        send(v_ref.at[pl.ds(0, 16)], svalues.at[pl.ds(0, 16)], vz_s.at[12 + oz], vz_r.at[oz - 1], at_z(oz), root)

    arrive(kchunk(x, z), sk_r.at[2], z > 0)
    for oz in (4, 5, 3, 6, 2, 7, 1):
        send(kchunk(x, z), kchunk(x, z), kz_s.at[oz - 1], kz_r.at[oz - 1], at_z(zpeer(oz)), (zpeer(oz) > 0) & has_prev)
        send(k_ref.at[pl.ds(0, 32), pl.ds(0, 128)], kchunk(0, 0), kz_s.at[20 + oz], kz_r.at[oz - 1], at_z(oz), root)
    for load in loads:
        load.wait()
    for load in sink_loads:
        pl.when(root)(lambda load=load: load.wait())

    @pl.when(root)
    def _():
        kv[0, BLK:2 * BLK] = jnp.zeros((BLK, HEADS * HDIM), BF)
        kv[1, BLK:2 * BLK] = jnp.zeros((BLK, HEADS * HDIM), BF)

    row = lax.broadcasted_iota(jnp.int32, (2 * BLK, 4 * BLK), 0)
    col = lax.broadcasted_iota(jnp.int32, (2 * BLK, 4 * BLK), 1)
    inside = lax.rem(col, BLK) <= lax.rem(row, BLK)
    col_blk, row_blk = lax.div(col, BLK), lax.div(row, BLK)
    first_shard = jnp.full((2 * BLK, 4 * BLK), c, jnp.int32) == 0
    keep = ((col_blk == 0) & (~first_shard | (row_blk == 1) | inside)) \
        | ((col_blk == 2) & (row_blk == 0) & inside & ~first_shard) \
        | ((col_blk == 3) & (row_blk == 1) & inside) \
        | (col_blk == row_blk + 1)
    bias[...] = jnp.where(keep, 0.0, MASKED)
    reach = pat[:, 1, :]
    block = lax.broadcasted_iota(jnp.int32, reach.shape, 1)
    for n in (0, 1):
        hit = (block == 2 * c + n) & (reach == 1) & (jnp.full(reach.shape, c, jnp.int32) > 0)
        on = jnp.max(jnp.where(hit, 1.0, 0.0), axis=1, keepdims=True)
        gate[n] = jnp.zeros((HEADS, 4 * BLK), F32)
        gate[n, :, (n + 1) * BLK:(n + 2) * BLK] = jnp.broadcast_to(jnp.where(on > 0.5, 0.0, MASKED), (HEADS, BLK))

    d_down, d_up, d_opp = down * 2 + core, up * 2 + core, opposite * 2 + core
    arrive(wrows(d_down, 0), w_r.at[0, 0])
    send(wrows(d_down, 0), wrows(d_down, 0), w_s.at[2, 0], w_r.at[2, 0], at_y(up))
    arrive(wrows(d_up, 1), w_r.at[1, 1])
    send(wrows(d_up, 1), wrows(d_up, 1), w_s.at[2, 1], w_r.at[2, 1], at_y(down))

    for oz in range(1, NZ):
        arrive(kchunk(x, zpeer(NZ - oz)), kz_r.at[oz - 1], z > 0)
    for o in (2, 1, 3):
        send(krows(skeys, x), krows(skeys, x), kx_s.at[o - 1], kx_r.at[o - 1], at_x(xpeer(o)), has_prev & ((z > 0) | (xpeer(o) > 0)))
        send(k_ref.at[pl.ds(0, 32)], skeys.at[pl.ds(0, 32)], kx_s.at[2 + o], kx_r.at[o - 1], at_x(o), root)

    def turn(n, carry):
        ct[lanes(n, 256), 0:256] = cot[:, lanes(n, 256)].T
        return carry

    lax.fori_loop(0, 8, turn, 0)

    arrive(wrows(d_down, 1), w_r.at[0, 1])
    send(wfull.at[lanes(d_down)], wfull.at[lanes(d_down)], core_s.at[2], core_r.at[2], at_core)
    arrive(wrows(d_up, 0), w_r.at[1, 0])
    send(wfull.at[lanes(d_up)], wfull.at[lanes(d_up)], core_s.at[3], core_r.at[3], at_core)

    arrive(cot_peer, core_r.at[1])

    def turn_peer(n, carry):
        ct[lanes(n, 256), 256:512] = cot_peer[:, lanes(n, 256)].T
        return carry

    lax.fori_loop(0, 8, turn_peer, 0)

    for o in range(1, NX):
        arrive(krows(skeys, xpeer(NX - o)), kx_r.at[o - 1], has_prev)
    for oz in range(1, NZ):
        arrive(vrows(svalues, zpeer(NZ - oz)), vz_r.at[oz - 1], has_prev)
    arrive(kv.at[0, pl.ds(BLK, BLK)], prev_r.at[0], has_prev)
    arrive(kv.at[1, pl.ds(BLK, BLK)], prev_r.at[1], has_prev)

    def forward(h):
        cols = lanes(h)
        s = dot(q[:, cols], kv[0, :, cols], 1, 1) * SCALE2 + bias[...]
        s = jnp.concatenate([s[0:BLK] + gate[0, pl.ds(h, 1), :], s[BLK:] + gate[1, pl.ds(h, 1), :]], axis=0)
        e = jnp.exp2(s - jnp.max(s, axis=1, keepdims=True))
        p = e * (1.0 / jnp.sum(e, axis=1, keepdims=True))
        return p, dot(p.astype(BF), kv[1, :, cols], 1, 0).astype(BF)

    def forward_some(j, parity):
        heads = [2 * (UNROLL * j + n) + parity for n in range(UNROLL)]
        done = [forward(h) for h in heads]
        for n, (p, out) in enumerate(done):
            probs[heads[n]] = p
            attn_all[:, lanes(heads[n])] = out
        return [(lanes(UNROLL * j + n), out) for n, (_, out) in enumerate(done)]

    def forward_other(j, carry):
        for place, out in forward_some(j, other):
            attn_send[:, place] = out
        return carry

    def forward_own(j, carry):
        for place, out in forward_some(j, core):
            a2[0:256, place] = out
        return carry

    lax.fori_loop(0, 4 // UNROLL, forward_other, 0)
    send(attn_send, a2.at[pl.ds(256, 256)], core_s.at[4], core_r.at[4], at_core)
    arrive(wrows(d_opp, 0), w_r.at[2, 0])
    arrive(wrows(d_opp, 1), w_r.at[2, 1])
    send(wfull.at[lanes(d_opp)], wfull.at[lanes(d_opp)], core_s.at[5], core_r.at[5], at_core)
    lax.fori_loop(0, 4 // UNROLL, forward_own, 0)

    arrive(a2.at[pl.ds(256, 256)], core_r.at[4])

    def partial(zz, carry):
        ptb[zz] = dot(ct[lanes(zz, 256), :], a2[...], 1, 0).astype(BF).reshape(NX, 64, 512)
        return carry

    xu, xd, xo = xpeer(1), xpeer(3), xpeer(2)

    def xpart(lo, xx):
        return ptb.at[pl.ds(lo, 2), xx]

    def ypart(lo, yy):
        return ptb.at[pl.ds(lo, 2), :, :, lanes(yy)]

    lax.fori_loop(0, 4, partial, 0)
    send(xpart(0, xo), xfwd.at[0], px_s.at[0], px_r.at[0], at_x(xu))
    send(xpart(2, xo), xfwd.at[1], px_s.at[1], px_r.at[1], at_x(xd))
    send(xpart(2, xu), xin.at[2], px_s.at[2], px_r.at[2], at_x(xu))
    send(xpart(0, xd), xin.at[3], px_s.at[3], px_r.at[3], at_x(xd))
    lax.fori_loop(4, 8, partial, 0)
    send(ypart(4, opposite), yfwd.at[0], py_s.at[0], py_r.at[0], at_y(up))
    send(ypart(6, opposite), yfwd.at[1], py_s.at[1], py_r.at[1], at_y(down))
    send(ypart(6, up), yin.at[2], py_s.at[2], py_r.at[2], at_y(up))
    send(ypart(4, down), yin.at[3], py_s.at[3], py_r.at[3], at_y(down))

    def peer_rows(dd):
        return wfull.at[lanes(dd)]

    arrive(peer_rows(y * 2 + other), core_r.at[0])
    arrive(peer_rows(down * 2 + other), core_r.at[2])
    arrive(peer_rows(up * 2 + other), core_r.at[3])
    arrive(peer_rows(opposite * 2 + other), core_r.at[5])

    def grad_attn(n, carry):
        grad[:, lanes(n, 256)] = dot(cot[...], wfull[lanes(n, 256), :], 1, 1).astype(BF)
        return carry

    lax.fori_loop(0, 4, grad_attn, 0)

    def backward_values(j, carry):
        places = [lanes(UNROLL * j + n) for n in range(UNROLL)]
        terms = [dot(probs[UNROLL * j + n].astype(BF), grad[:, cols], 0, 0) for n, cols in enumerate(places)]
        for cols, term in zip(places, terms):
            sgv[:, cols] = term[0:128].astype(BF)
            pg[1, :, cols] = term[128:256].astype(BF)
            acc[1, :, cols] = term[256:512]
        return carry

    lax.fori_loop(0, HEADS // UNROLL, backward_values, 0)
    for oz in (4, 5, 3, 6, 2, 7, 1):
        send(vrows(sgv, zpeer(oz)), gv1.at[oz - 1], gv1_s.at[oz - 1], gv1_r.at[oz - 1], at_z(zpeer(oz)))

    def merge(fwd, part):
        return (fwd.astype(F32) + part.astype(F32)).astype(BF)

    arrive(xfwd.at[0], px_r.at[0])
    xmrg[0] = merge(xfwd[0], ptb[0:2, xu])
    send(xmrg.at[0], xin.at[0], px_s.at[4], px_r.at[4], at_x(xu))
    arrive(xfwd.at[1], px_r.at[1])
    xmrg[1] = merge(xfwd[1], ptb[2:4, xd])
    send(xmrg.at[1], xin.at[1], px_s.at[5], px_r.at[5], at_x(xd))
    arrive(yfwd.at[0], py_r.at[0])
    ymrg[0] = merge(yfwd[0], ptb[4:6, :, :, lanes(up)])
    send(ymrg.at[0], yin.at[0], py_s.at[4], py_r.at[4], at_y(up))
    arrive(yfwd.at[1], py_r.at[1])
    ymrg[1] = merge(yfwd[1], ptb[6:8, :, :, lanes(down)])
    send(ymrg.at[1], yin.at[1], py_s.at[5], py_r.at[5], at_y(down))
    send(pg.at[1], pg_recv.at[1], pg_s.at[1], pg_r.at[1], (c - 1, d), has_prev)

    def backward_head(h):
        cols = lanes(h)
        g = grad[:, cols]
        delta = jnp.sum(g.astype(F32) * attn_all[:, cols].astype(F32), axis=1, keepdims=True)
        ds = (probs[h] * (dot(g, kv[1, :, cols], 1, 1) - delta)).astype(BF)
        return cols, dot(ds, q[:, cols], 0, 0) * SCALE, (dot(ds, kv[0, :, cols], 1, 0) * SCALE).astype(BF)

    def backward(j, carry):
        for cols, term, query_grad in [backward_head(UNROLL * j + n) for n in range(UNROLL)]:
            sgk[:, cols] = term[0:128].astype(BF)
            pg[0, :, cols] = term[128:256].astype(BF)
            acc[0, :, cols] = term[256:512]
            dq_ref[:, cols] = query_grad
        return carry

    lax.fori_loop(0, HEADS // UNROLL, backward, 0)
    for o in (2, 1, 3):
        send(krows(sgk, xpeer(o)), gk1.at[o - 1], gk1_s.at[o - 1], gk1_r.at[o - 1], at_x(xpeer(o)))

    for oz in range(1, NZ):
        arrive(gv1.at[oz - 1], gv1_r.at[oz - 1])
    total = sgv[pl.ds(pl.multiple_of(z * 16, 16), 16), :].astype(F32)
    for oz in range(1, NZ):
        total += gv1[oz - 1].astype(F32)
    gv1s[...] = total.astype(BF)
    send(gv1s, gv2.at[x], gv2_s, gv2_r.at[x], at_x(0), x > 0)

    arrive(xin.at[0], px_r.at[4])
    arrive(xin.at[3], px_r.at[3])
    arrive(xin.at[1], px_r.at[5])
    arrive(xin.at[2], px_r.at[2])
    for half in (0, 1):
        both = slice(2 * half, 2 * half + 2)
        s2x[both] = (ptb[both, x].astype(F32) + xin[half].astype(F32) + xin[3 - half].astype(F32)).astype(BF)
    for o in (2, 1, 3):
        send(s2x.at[:, :, lanes(ypeer(o))], r2y.at[o - 1], p2_s.at[o - 1], p2_r.at[o - 1], at_y(ypeer(o)))
    arrive(yin.at[0], py_r.at[4])
    arrive(yin.at[3], py_r.at[3])
    arrive(yin.at[1], py_r.at[5])
    arrive(yin.at[2], py_r.at[2])
    for half in (0, 1):
        both, here = slice(4 + 2 * half, 6 + 2 * half), slice(2 * half, 2 * half + 2)
        s2y[here] = (ptb[both, :, :, lanes(y)].astype(F32) + yin[half].astype(F32) + yin[3 - half].astype(F32)).astype(BF)
    for o in (2, 1, 3):
        send(s2y.at[:, xpeer(o)], r2x.at[o - 1], p2_s.at[o + 2], p2_r.at[o + 2], at_x(xpeer(o)))

    for o in range(1, NX):
        arrive(gk1.at[o - 1], gk1_r.at[o - 1])
    total = sgk[pl.ds(pl.multiple_of(x * 32, 32), 32), :].astype(F32)
    for o in range(1, NX):
        total += gk1[o - 1].astype(F32)
    gk1s[...] = total.astype(BF)
    send(gk1s, gk2.at[z], gk2_s, gk2_r.at[z], at_z(0), z > 0)

    @pl.when(col0)
    def _():
        for xx in range(1, NX):
            arrive(gv2.at[xx], gv2_r.at[xx])
        total = gv1s[...].astype(F32)
        for xx in range(1, NX):
            total += gv2[xx].astype(F32)
        gv2s[...] = total.astype(BF)

    send(gv2s, gv3.at[z], gv3_s, gv3_r.at[z], at_z(0), col0 & has_prev)

    def project(n, carry):
        proj_ref[:, lanes(n, 256)] = dot(attn_all[...], wfull[:, lanes(n, 256)], 1, 0).astype(BF)
        return carry

    lax.fori_loop(0, 4, project, 0)

    for o in range(1, NX):
        arrive(r2y.at[o - 1], p2_r.at[o - 1])
    total = s2x[:, :, lanes(y)].astype(F32)
    for o in range(1, NY):
        total += r2y[o - 1].astype(F32)
    red[0:4] = total.astype(BF)
    for o in range(1, NX):
        arrive(r2x.at[o - 1], p2_r.at[o + 2])
    total = s2y[:, x].astype(F32)
    for o in range(1, NX):
        total += r2x[o - 1].astype(F32)
    red[4:8] = total.astype(BF)
    for oz in (4, 5, 3, 6, 2, 7, 1):
        send(red.at[zpeer(oz)], r3.at[oz - 1], p3_s.at[oz - 1], p3_r.at[oz - 1], at_z(zpeer(oz)))
    send(pg.at[0], pg_recv.at[0], pg_s.at[0], pg_r.at[0], (c - 1, d), has_prev)

    @pl.when(row0)
    def _():
        for zz in range(1, NZ):
            arrive(gk2.at[zz], gk2_r.at[zz])
        total = gk1s[...].astype(F32)
        for zz in range(1, NZ):
            total += gk2[zz].astype(F32)
        gk2s[...] = total.astype(BF)

    send(gk2s, gk3.at[x], gk3_s, gk3_r.at[x], at_x(0), row0 & has_prev)

    lax.fori_loop(4, 8, project, 0)

    for n, out_ref in ((1, dv_ref), (0, dk_ref)):
        arrive(pg_recv.at[n], pg_r.at[n], has_next)
        out_ref[0:BLK] = acc[n, 0:BLK].astype(BF)

        @pl.when(has_next)
        def _(n=n, out_ref=out_ref):
            out_ref[BLK:] = (acc[n, BLK:] + pg_recv[n].astype(F32)).astype(BF)

        @pl.when(jnp.logical_not(has_next))
        def _(n=n, out_ref=out_ref):
            out_ref[BLK:] = acc[n, BLK:].astype(BF)

    for oz in range(1, NZ):
        arrive(r3.at[oz - 1], p3_r.at[oz - 1])
    total = red[z].astype(F32)
    for oz in range(1, NZ):
        total += r3[oz - 1].astype(F32)
    gp_ref[...] = total * (1.0 / 256.0)

    @pl.when(root)
    def _():
        for zz in range(1, NZ):
            arrive(gv3.at[zz], gv3_r.at[zz])
        for zz in range(NZ):
            rows = slice(16 * zz, 16 * zz + 16)
            part = gv2s[...] if zz == 0 else gv3[zz]
            dv_ref[rows] = (acc[1, rows] + part.astype(F32)).astype(BF)
        for xx in range(1, NX):
            arrive(gk3.at[xx], gk3_r.at[xx])
        for xx in range(NX):
            rows = slice(32 * xx, 32 * xx + 32)
            part = gk2s[...] if xx == 0 else gk3[xx]
            dk_ref[rows] = (acc[0, rows] + part.astype(F32)).astype(BF)

    for cond, copy in pending:
        if cond is None:
            copy.wait_send()
        else:
            pl.when(cond)(lambda copy=copy: copy.wait_send())


def store(*refs):
    count = (len(refs) - 1) // 2
    copies = [pltpu.make_async_copy(refs[n], refs[count + n], refs[-1].at[n]) for n in range(count)]
    for copy in copies:
        copy.start()
    for copy in copies:
        copy.wait()


def body(queries, keys, values, cotangent, proj_weight, pattern):
    rows, width = queries.shape[1:]
    full = cotangent.shape[2]
    vmem, hbm = pl.BlockSpec(memory_space=pltpu.VMEM), pl.BlockSpec(memory_space=pltpu.HBM)
    V, D = pltpu.VMEM, pltpu.SemaphoreType.DMA
    scratch = [
        V((HEADS, 2, 64), jnp.int32), V((rows, width), BF), V((rows, full), BF),
        V((1024, full), BF), V((2, 512, width), BF), V((full, 512), BF), V((rows, full), BF),
        V((512, 512), BF), V((rows, 512), BF), V((rows, width), BF), V((rows, width), BF),
        V((2, HEADS, 4 * BLK), F32), V((256, 512), F32), V((HEADS, 256, 512), F32),
        V((2, 256, width), F32), V((2, 128, width), BF), V((2, 128, width), BF),
        V((128, width), BF), V((3, 32, width), BF), V((32, width), BF), V((8, 32, width), BF), V((32, width), BF), V((4, 32, width), BF),
        V((128, width), BF), V((7, 16, width), BF), V((16, width), BF), V((4, 16, width), BF), V((16, width), BF), V((8, 16, width), BF),
        V((8, 4, 64, 512), BF),
        V((2, 2, 64, 512), BF), V((2, 2, 64, 512), BF), V((4, 2, 64, 512), BF),
        V((2, 2, 4, 64, 128), BF), V((2, 2, 4, 64, 128), BF), V((4, 2, 4, 64, 128), BF),
        V((4, 64, 512), BF), V((4, 4, 64, 128), BF), V((3, 4, 64, 128), BF), V((3, 4, 64, 128), BF),
        V((8, 64, 128), BF), V((7, 64, 128), BF),
        D((8,)), D((3,)), D((2,)), D((3, 2)), D((3, 2)), D((6,)), D((6,)), D((11,)), D((4,)), D((28,)), D((7,)), D((6,)), D((3,)),
        D((20,)), D((7,)),
        D((2,)), D((2,)), D((3,)), D((3,)), D, D((8,)), D, D((4,)), D((7,)), D((7,)), D, D((4,)), D, D((8,)),
        D((6,)), D((6,)), D((6,)), D((6,)), D((6,)), D((6,)), D((7,)), D((7,)),
    ]
    shapes = [((rows, full), BF), ((rows, width), BF), ((rows, width), BF), ((rows, width), BF), ((64, 128), F32)]
    outs = pl.pallas_call(
        kernel,
        out_shape=[pltpu.VMEM(*s) for s in shapes],
        in_specs=[hbm] * 6,
        out_specs=[vmem] * 5,
        scratch_shapes=scratch,
        compiler_params=pltpu.CompilerParams(
            collective_id=0, has_side_effects=True, vmem_limit_bytes=58 * 1024 * 1024
        ),
        cost_estimate=pl.CostEstimate(flops=4_400_000_000, bytes_accessed=6_500_000, transcendentals=1_000_000),
    )(jnp.swapaxes(pattern, 2, 3)[0], queries[0], keys[0], values[0], cotangent[0], proj_weight)
    proj, dq, dk, dv, gp = pl.pallas_call(
        store,
        out_shape=[jax.ShapeDtypeStruct(*s) for s in shapes],
        in_specs=[pl.BlockSpec(memory_space=pl.ANY)] * 5,
        out_specs=[hbm] * 5,
        scratch_shapes=[D((5,))],
        compiler_params=pltpu.CompilerParams(vmem_limit_bytes=1024 * 1024),
    )(*outs)
    return proj[None], dq[None], dk[None], dv[None], gp.T


def solution(mesh):
    return jax.shard_map(
        body,
        mesh=mesh,
        in_specs=(
            P("dp", "ctx", None),
            P("dp", "ctx", None),
            P("dp", "ctx", None),
            P("dp", "ctx", None),
            P("dp", None),
            P("dp", None, None, None),
        ),
        out_specs=(
            P("dp", "ctx", None),
            P("dp", "ctx", None),
            P("dp", "ctx", None),
            P("dp", "ctx", None),
            P("dp", "ctx"),
        ),
        check_vma=False,
    )
```

time: 608 us -> 78.1 us (0.13)
  waiting for transfers between devices: 489 us -> 0 us
  Pallas kernels: 0 us -> 77.4 us
  local copies, waits for them, and re-layouts: 43.7 us -> 0 us
  matrix products: 24.8 us -> 0 us
  other arithmetic: 16.5 us -> 0 us
  between operations: 15.7 us -> 0.64 us
  starting transfers between devices: 13.3 us -> 0 us
    reduce_scatter x2 -> x0, waiting for transfers between devices: 243 us -> none  [the longest x1 217 us: body(): lax.psum_scatter(weight_term, 'ctx', scatter_dimension=1, tiled=True)]
    psum x2 -> x0, waiting for transfers between devices: 230 us -> none  [the longest x1 118 us: spread(): return lax.psum(block, axis)]
    pallas_call x0 -> x2, Pallas kernels: none -> 77.4 us  [the longest x1 75.9 us: body(): pl.pallas_call(kernel, out_shape=[pltpu.VMEM(*s) for s in shapes], in_spe...]
    dot_general x15 -> x0, matrix products: 24.8 us -> none  [the longest x12 14.5 us: product(): return jnp.einsum(form, left, right, preferred_element_type=jnp.float32)]
    ppermute x4 -> x0, waiting for transfers between devices: 15.3 us -> none  [shifted(): lax.ppermute(value, axis, [(source, source + steps) for source in range(l...]
    ppermute x4 -> x0, starting transfers between devices: 12.9 us -> none  [shifted(): lax.ppermute(value, axis, [(source, source + steps) for source in range(l...]
    unnamed x69 -> x0, local copies, waits for them, and re-layouts: 12 us -> none
    add x6 -> x0, other arithmetic: 7.03 us -> none  [the longest x2 3.21 us: place_windows(): placed + jnp.pad(flat[number], (((number + 1) * BLK, (2 * BLK_DEV - numbe...]
  transfers between devices with their start and end apart: 9 -> 0, of which waited for: 6 -> 0; matrix products, arithmetic and copies ran while one was open for 10% -> 0% of each run, Pallas kernels for 0% -> 0%
where the time goes in v1:
time: 78.1 us
  Pallas kernels  77.4 us (99%)
    pallas_call x1, Pallas kernels, body(): pl.pallas_call(kernel, out_shape=[pltpu.VMEM(*s) for s in shapes], in_spe...  75.9 us

profile of v1, /device:TPU:14, one launch (start us, length us, event | category | flops | bytes accessed | tf_op | source)
XLA Modules:
  0.0 78.1 jit_solution(17005970916968531701)
XLA Ops:
  0.6 75.9 %shard_map.101 = (bf16[256,2048]{1,0:T(8,128)(2,1)S(1)}, bf16[256,1024]{1,0:T(8,128)(2,1)S(1)}, bf16[256,1024]{1,0:T(8,128)(2,1)S(1)}, bf16[256,1024]{1,0:T(8,128)(2,1)S(1)}, f32[64,128]{1,0:T(8,128)S(1)}) custom-call(s32[8,2,64]{2,1,0:T(2,128)} %bitcast.21, bf16[256,1024]{1,0:T(8,128)(2,1)} %bitcast.14, bf16[256,1024]{1,0:T(8,128)(2,1)} %bitcast.15, ...), custom_call_target="tpu_custom_call" | custom-call | flops 4400000000 | bytes 6500000 | tf_op jit(solution)/shard_map/pallas_call | solution.py:509
  76.5 1.5 %shard_map.102 = (bf16[256,2048]{1,0:T(8,128)(2,1)}, bf16[256,1024]{1,0:T(8,128)(2,1)}, bf16[256,1024]{1,0:T(8,128)(2,1)}, bf16[256,1024]{1,0:T(8,128)(2,1)}, f32[64,128]{1,0:T(8,128)}) custom-call(bf16[256,2048]{1,0:T(8,128)(2,1)S(1)} %get-tuple-element.15.refs_0_, bf16[256,1024]{1,0:T(8,128)(2,1)S(1)} %get-tuple-element.16.refs_1_, ...), custom_call_target="tpu_custom_call" | custom-call | tf_op jit(solution)/shard_map/pallas_call | solution.py:520

commit v2 on v1

--- a/solution.py
+++ b/solution.py
@@ -147,6 +147,10 @@
              kchunk(x, oz), kz_s.at[6 + oz], sk_r.at[2], at_z(oz), row0 & has_prev)
         send(k_ref.at[pl.ds(0, 32), pl.ds(oz * 128, 128)], kchunk(0, oz), kz_s.at[13 + oz], sk_r.at[2], at_z(oz), root)
     send(k_ref.at[pl.ds(BLK, BLK)], kv.at[0, pl.ds(BLK, BLK)], prev_s.at[2], prev_r.at[0], (c + 1, d), row0)
+    arrive(kchunk(x, z), sk_r.at[2], z > 0)
+    for oz in (4, 5, 3, 6, 2, 7, 1):
+        send(kchunk(x, z), kchunk(x, z), kz_s.at[oz - 1], kz_r.at[oz - 1], at_z(zpeer(oz)), (zpeer(oz) > 0) & has_prev)
+        send(k_ref.at[pl.ds(0, 32), pl.ds(0, 128)], kchunk(0, 0), kz_s.at[20 + oz], kz_r.at[oz - 1], at_z(oz), root)
     arrive(vrows(svalues, z), sk_r.at[1], col0 & has_prev)
     for o in (2, 1, 3):
         send(vrows(svalues, z), vrows(svalues, z), vz_s.at[6 + o], sk_r.at[3], at_x(o), col0 & has_prev)
@@ -160,10 +164,6 @@
              has_prev & ((x > 0) | (zpeer(oz) > 0)))
         send(v_ref.at[pl.ds(0, 16)], svalues.at[pl.ds(0, 16)], vz_s.at[12 + oz], vz_r.at[oz - 1], at_z(oz), root)
 
-    arrive(kchunk(x, z), sk_r.at[2], z > 0)
-    for oz in (4, 5, 3, 6, 2, 7, 1):
-        send(kchunk(x, z), kchunk(x, z), kz_s.at[oz - 1], kz_r.at[oz - 1], at_z(zpeer(oz)), (zpeer(oz) > 0) & has_prev)
-        send(k_ref.at[pl.ds(0, 32), pl.ds(0, 128)], kchunk(0, 0), kz_s.at[20 + oz], kz_r.at[oz - 1], at_z(oz), root)
     for load in loads:
         load.wait()
     for load in sink_loads:

time: 78.1 us -> 72.2 us (0.924)
  Pallas kernels: 77.4 us -> 71.1 us
    pallas_call x1, Pallas kernels: 75.9 us -> 69.5 us  [body(): pl.pallas_call(kernel, out_shape=[pltpu.VMEM(*s) for s in shapes], in_spe...]
where the time goes in v2:
time: 72.2 us; the launch traced here: 71.7 us
  Pallas kernels  71.1 us (98%)
    pallas_call x1, Pallas kernels, body(): pl.pallas_call(kernel, out_shape=[pltpu.VMEM(*s) for s in shapes], in_spe...  69.5 us
    pallas_call x1, Pallas kernels, body(): pl.pallas_call(store, out_shape=[jax.ShapeDtypeStruct(*s) for s in shapes...  1.53 us

profile of v2, /device:TPU:14, one launch (start us, length us, event | category | flops | bytes accessed | tf_op | source)
XLA Modules:
  0.0 71.7 jit_solution(14111025276685417876)
XLA Ops:
  0.6 69.5 %shard_map.101 = (bf16[256,2048]{1,0:T(8,128)(2,1)S(1)}, bf16[256,1024]{1,0:T(8,128)(2,1)S(1)}, bf16[256,1024]{1,0:T(8,128)(2,1)S(1)}, bf16[256,1024]{1,0:T(8,128)(2,1)S(1)}, f32[64,128]{1,0:T(8,128)S(1)}) custom-call(s32[8,2,64]{2,1,0:T(2,128)} %bitcast.21, bf16[256,1024]{1,0:T(8,128)(2,1)} %bitcast.14, bf16[256,1024]{1,0:T(8,128)(2,1)} %bitcast.15, ...), custom_call_target="tpu_custom_call" | custom-call | flops 4400000000 | bytes 6500000 | tf_op jit(solution)/shard_map/pallas_call | solution.py:509
  70.2 1.5 %shard_map.102 = (bf16[256,2048]{1,0:T(8,128)(2,1)}, bf16[256,1024]{1,0:T(8,128)(2,1)}, bf16[256,1024]{1,0:T(8,128)(2,1)}, bf16[256,1024]{1,0:T(8,128)(2,1)}, f32[64,128]{1,0:T(8,128)}) custom-call(bf16[256,2048]{1,0:T(8,128)(2,1)S(1)} %get-tuple-element.15.refs_0_, bf16[256,1024]{1,0:T(8,128)(2,1)S(1)} %get-tuple-element.16.refs_1_, ...), custom_call_target="tpu_custom_call" | custom-call | tf_op jit(solution)/shard_map/pallas_call | solution.py:520

commit v3 on v2

--- a/solution.py
+++ b/solution.py
@@ -78,6 +78,14 @@
             copy.wait_recv()
         else:
             pl.when(cond)(lambda: copy.wait_recv())
+
+    def drain(count):
+        for cond, copy in pending[:count]:
+            if cond is None:
+                copy.wait_send()
+            else:
+                pl.when(cond)(lambda copy=copy: copy.wait_send())
+        del pending[:count]
 
     own = pl.ds(2 * BLK, 2 * BLK)
     loads = [
@@ -332,6 +340,8 @@
     send(ymrg.at[1], yin.at[1], py_s.at[5], py_r.at[5], at_y(down))
     send(pg.at[1], pg_recv.at[1], pg_s.at[1], pg_r.at[1], (c - 1, d), has_prev)
 
+    sent_early = len(pending)
+
     def backward_head(h):
         cols = lanes(h)
         g = grad[:, cols]
@@ -358,6 +368,16 @@
         total += gv1[oz - 1].astype(F32)
     gv1s[...] = total.astype(BF)
     send(gv1s, gv2.at[x], gv2_s, gv2_r.at[x], at_x(0), x > 0)
+
+    arrive(yin.at[0], py_r.at[4])
+    arrive(yin.at[3], py_r.at[3])
+    arrive(yin.at[1], py_r.at[5])
+    arrive(yin.at[2], py_r.at[2])
+    for half in (0, 1):
+        both, here = slice(4 + 2 * half, 6 + 2 * half), slice(2 * half, 2 * half + 2)
+        s2y[here] = (ptb[both, :, :, lanes(y)].astype(F32) + yin[half].astype(F32) + yin[3 - half].astype(F32)).astype(BF)
+    for o in (2, 1, 3):
+        send(s2y.at[:, xpeer(o)], r2x.at[o - 1], p2_s.at[o + 2], p2_r.at[o + 2], at_x(xpeer(o)))
 
     arrive(xin.at[0], px_r.at[4])
     arrive(xin.at[3], px_r.at[3])
@@ -368,15 +388,6 @@
         s2x[both] = (ptb[both, x].astype(F32) + xin[half].astype(F32) + xin[3 - half].astype(F32)).astype(BF)
     for o in (2, 1, 3):
         send(s2x.at[:, :, lanes(ypeer(o))], r2y.at[o - 1], p2_s.at[o - 1], p2_r.at[o - 1], at_y(ypeer(o)))
-    arrive(yin.at[0], py_r.at[4])
-    arrive(yin.at[3], py_r.at[3])
-    arrive(yin.at[1], py_r.at[5])
-    arrive(yin.at[2], py_r.at[2])
-    for half in (0, 1):
-        both, here = slice(4 + 2 * half, 6 + 2 * half), slice(2 * half, 2 * half + 2)
-        s2y[here] = (ptb[both, :, :, lanes(y)].astype(F32) + yin[half].astype(F32) + yin[3 - half].astype(F32)).astype(BF)
-    for o in (2, 1, 3):
-        send(s2y.at[:, xpeer(o)], r2x.at[o - 1], p2_s.at[o + 2], p2_r.at[o + 2], at_x(xpeer(o)))
 
     for o in range(1, NX):
         arrive(gk1.at[o - 1], gk1_r.at[o - 1])
@@ -403,6 +414,8 @@
 
     lax.fori_loop(0, 4, project, 0)
 
+    drain(sent_early)
+
     for o in range(1, NX):
         arrive(r2y.at[o - 1], p2_r.at[o - 1])
     total = s2x[:, :, lanes(y)].astype(F32)
@@ -432,24 +445,24 @@
 
     lax.fori_loop(4, 8, project, 0)
 
-    for n, out_ref in ((1, dv_ref), (0, dk_ref)):
-        arrive(pg_recv.at[n], pg_r.at[n], has_next)
-        out_ref[0:BLK] = acc[n, 0:BLK].astype(BF)
-
-        @pl.when(has_next)
-        def _(n=n, out_ref=out_ref):
-            out_ref[BLK:] = (acc[n, BLK:] + pg_recv[n].astype(F32)).astype(BF)
-
-        @pl.when(jnp.logical_not(has_next))
-        def _(n=n, out_ref=out_ref):
-            out_ref[BLK:] = acc[n, BLK:].astype(BF)
-
     for oz in range(1, NZ):
         arrive(r3.at[oz - 1], p3_r.at[oz - 1])
     total = red[z].astype(F32)
     for oz in range(1, NZ):
         total += r3[oz - 1].astype(F32)
     gp_ref[...] = total * (1.0 / 256.0)
+
+    for n, out_ref in ((1, dv_ref), (0, dk_ref)):
+        arrive(pg_recv.at[n], pg_r.at[n], has_next)
+        out_ref[0:BLK] = acc[n, 0:BLK].astype(BF)
+
+        @pl.when(has_next)
+        def _(n=n, out_ref=out_ref):
+            out_ref[BLK:] = (acc[n, BLK:] + pg_recv[n].astype(F32)).astype(BF)
+
+        @pl.when(jnp.logical_not(has_next))
+        def _(n=n, out_ref=out_ref):
+            out_ref[BLK:] = acc[n, BLK:].astype(BF)
 
     @pl.when(root)
     def _():
@@ -466,11 +479,7 @@
             part = gk2s[...] if xx == 0 else gk3[xx]
             dk_ref[rows] = (acc[0, rows] + part.astype(F32)).astype(BF)
 
-    for cond, copy in pending:
-        if cond is None:
-            copy.wait_send()
-        else:
-            pl.when(cond)(lambda copy=copy: copy.wait_send())
+    drain(len(pending))
 
 
 def store(*refs):

time: 72.2 us -> 72.2 us (level)
  no operation moved by 1% of the time
where the time goes in v3:
time: 72.2 us; the launch traced here: 71.5 us
  Pallas kernels  70.9 us (98%)
    pallas_call x1, Pallas kernels, body(): pl.pallas_call(kernel, out_shape=[pltpu.VMEM(*s) for s in shapes], in_spe...  69.3 us
    pallas_call x1, Pallas kernels, body(): pl.pallas_call(store, out_shape=[jax.ShapeDtypeStruct(*s) for s in shapes...  1.53 us

profile of v3, /device:TPU:14, one launch (start us, length us, event | category | flops | bytes accessed | tf_op | source)
XLA Modules:
  0.0 71.5 jit_solution(5115693081918070027)
XLA Ops:
  0.6 69.3 %shard_map.101 = (bf16[256,2048]{1,0:T(8,128)(2,1)S(1)}, bf16[256,1024]{1,0:T(8,128)(2,1)S(1)}, bf16[256,1024]{1,0:T(8,128)(2,1)S(1)}, bf16[256,1024]{1,0:T(8,128)(2,1)S(1)}, f32[64,128]{1,0:T(8,128)S(1)}) custom-call(s32[8,2,64]{2,1,0:T(2,128)} %bitcast.21, bf16[256,1024]{1,0:T(8,128)(2,1)} %bitcast.14, bf16[256,1024]{1,0:T(8,128)(2,1)} %bitcast.15, ...), custom_call_target="tpu_custom_call" | custom-call | flops 4400000000 | bytes 6500000 | tf_op jit(solution)/shard_map/pallas_call | solution.py:518
  70.0 1.5 %shard_map.102 = (bf16[256,2048]{1,0:T(8,128)(2,1)}, bf16[256,1024]{1,0:T(8,128)(2,1)}, bf16[256,1024]{1,0:T(8,128)(2,1)}, bf16[256,1024]{1,0:T(8,128)(2,1)}, f32[64,128]{1,0:T(8,128)}) custom-call(bf16[256,2048]{1,0:T(8,128)(2,1)S(1)} %get-tuple-element.15.refs_0_, bf16[256,1024]{1,0:T(8,128)(2,1)S(1)} %get-tuple-element.16.refs_1_, ...), custom_call_target="tpu_custom_call" | custom-call | tf_op jit(solution)/shard_map/pallas_call | solution.py:529
